TPU v7x, 256 devices: a whole 4x4x8 slice. The times are simulated.
256 devices in a mesh: rep: 8 (over x_hi, y), fsdp: 32 (over z, x_lo, core).
Axes of the slice: x: 4 (x_hi: 2, x_lo: 2; x = x_hi * 2 + x_lo), y: 4, z: 8, core: 2. Of those that a mesh axis runs over, the one named last changes fastest.
Arguments:
- deltas: bfloat16 [8, 2, 1024, 8192], P('rep', None, 'fsdp'), may hold values from -2.5 to 2.5
- residual: bfloat16 [8, 2, 1024, 8192], P('rep', None, 'fsdp'), may hold values from -2.5 to 2.5
- params: float32 [2, 1024, 8192], P(None, 'fsdp'), may hold values from -6 to 6
- momentum: float32 [2, 1024, 8192], P(None, 'fsdp'), may hold values from -4 to 4
- left_sketch: bfloat16 [1024, 512], P('fsdp'), may hold values from -0.25 to 0.25
- right_hash: int32 [8192], replicated, may hold values from 0 to 1023
Outputs:
- new_params: float32 [2, 1024, 8192], P(None, 'fsdp')
- new_momentum: float32 [2, 1024, 8192], P(None, 'fsdp')
- new_residual: bfloat16 [8, 2, 1024, 8192], P('rep', None, 'fsdp')
Inputs may be any that keep to these rules, and one draw needn't show every extreme that they name: right_hash % 512 is a column's bucket and right_hash // 512 (0 or 1) its sign bit.
All inputs are finite; a program needn't handle non-finite values.
Results may differ from a plain program's by a relative error of at most 0.0013.
Values sent between devices are 32-bit elements; how exact they have to be, the bound alone decides.
No kernel may reach another device: no remote copies, remote signals or barrier semaphores. Data moves between devices by JAX's collectives and lax.ppermute only.
A program may use at most 64 MiB of HBM per device.

v0:
```python
import jax
import jax.numpy as jnp
from jax import lax
from jax.sharding import PartitionSpec as P

K2 = 512


def signed_table(right_hash, buckets):
    bucket_ids = right_hash % buckets
    column_signs = (1 - 2 * (right_hash // buckets)).astype(jnp.float32)
    columns = jnp.arange(buckets, dtype=jnp.int32)
    return jnp.where(
        bucket_ids[:, None] == columns[None, :], column_signs[:, None], jnp.float32(0.0)
    )


def per_device(deltas, residual, params, momentum, left_sketch, right_hash):
    highest = lax.Precision.HIGHEST
    accumulated = residual.astype(jnp.float32) + deltas.astype(jnp.float32)
    signed = signed_table(right_hash, K2)
    projections = accumulated.shape[1]
    row_count = accumulated.shape[2]
    local_y = jnp.einsum("pmn,nk->mpk", accumulated[0], signed, precision=highest)
    local_y = local_y.reshape(row_count, projections * K2)
    left_wide = left_sketch.astype(jnp.float32)
    replicas = lax.axis_size("rep")
    partial_sketch = jnp.dot(left_wide.T, local_y, precision=highest)
    total_sketch = lax.psum(partial_sketch, ("rep", "fsdp")) / replicas
    projected = jnp.dot(left_wide, total_sketch, precision=highest)
    projected = projected.reshape(row_count, projections, K2)
    update = jnp.einsum("mpk,nk->pmn", projected, signed, precision=highest)
    new_residual = (accumulated - update[None]).astype(jnp.bfloat16)
    new_momentum = 0.9 * momentum + update
    new_params = params - 0.7 * (update + 0.9 * new_momentum)
    return (new_params, new_momentum, new_residual)


def solution(mesh):
    in_specs = (
        P("rep", None, "fsdp", None),
        P("rep", None, "fsdp", None),
        P(None, "fsdp", None),
        P(None, "fsdp", None),
        P("fsdp", None),
        P(),
    )
    out_specs = (P(None, "fsdp", None), P(None, "fsdp", None), P("rep", None, "fsdp", None))
    return jax.shard_map(
        per_device, mesh=mesh, in_specs=in_specs, out_specs=out_specs, check_vma=False
    )
```

profile of v0, /device:TPU:1, one launch (start us, length us, event | category | flops | bytes accessed | tf_op | source)
XLA Modules:
  0.0 319.5 jit_solution(16081726443631032472)
XLA Ops:
  7.2 0.0 copy-start
  7.2 0.0 all-reduce.2.cloned.1.call-start
  7.2 0.8 add_select_fusion.1
  8.0 14.0 %fusion.18 = f32[2,4,8,512]{3,2,1,0:T(8,128)S(1)} fusion(bf16[1,2,32,8192]{3,2,1,0:T(8,128)(2,1)} %param.6, bf16[1,2,32,8192]{3,2,1,0:T(8,128)(2,1)} %param.7, f32[8192]{0:T(1024)S(1)} %get-tuple-element.6, s32[8192]{0:T(1024)S(1)} %get-tuple-element.5), kind=kOutput, calls=%fused_computation.24 | convolution fusion | flops 3231186944 | bytes 2293760 | tf_op jit(solution)/shard_map/pmn,nk->mpk/dot_general | solution.py:24
  22.1 0.0 copy-done
  22.1 2.4 convolution_bitcast_fusion
  24.4 0.0 copy-start.3
  24.4 0.0 all-reduce.2.cloned.1.call-update
  24.5 263.7 %all-reduce.2.cloned.1.call-done = f32[512,1024]{0,1:T(8,128)} async-done(((f32[512,1024]{0,1:T(8,128)}), f32[512,1024]{0,1:T(8,128)}) %all-reduce.2.cloned.1.call-update) | async-done | bytes 2097168 | tf_op jit(solution)/shard_map/psum | solution.py:29
  288.2 0.0 copy-start.4
  288.2 3.1 fusion.16
  291.3 0.0 copy-done.3
  291.3 0.0 copy-done.4
  291.3 0.0 copy-start.1
  291.3 0.0 copy-start.2
  291.3 20.1 %fusion.14 = (f32[2,32,8192]{2,1,0:T(8,128)}, f32[2,32,8192]{2,1,0:T(8,128)}, f32[8192,32,2]{0,1,2:T(8,128)S(1)}) fusion(f32[2,32,8192]{2,1,0:T(8,128)S(1)} %copy-done.3, f32[2,32,8192]{2,1,0:T(8,128)S(1)} %copy-done.4, f32[4,2,8,512]{3,2,1,0:T(8,128)S(1)} %bitcast.44, f32[8192]{0:T(1024)S(1)} %get-tuple-element.6, s32[8192]{0:T(1024)S(1)} %get-tuple-element.5), kind=kOutput, calls=%fused_computation.18 | convolution fusion | flops 3232759808 | bytes 10682368 | tf_op jit(solution)/shard_map/mpk,nk->pmn/dot_general | solution.py:32
  311.4 0.0 copy-done.1
  311.4 0.0 copy-done.2
  311.4 1.3 fusion.12
  (1 shorter events, 0.0 us)
Async XLA Ops:
  7.2 14.9 %copy-start = (bf16[32,512]{1,0:T(8,128)(2,1)S(1)}, bf16[32,512]{1,0:T(8,128)(2,1)}, u32[]{:S(2)}) copy-start(bf16[32,512]{1,0:T(8,128)(2,1)} %param.10) | copy-start | bytes 98308
  7.2 281.0 %all-reduce.2.cloned.1.call-start = ((), (), s32[]{:S(2)}) async-start(), calls=%async_computation | async-start | bytes 4194304 | tf_op jit(solution)/shard_map/psum | solution.py:29
  24.4 266.9 %copy-start.3 = (f32[2,32,8192]{2,1,0:T(8,128)S(1)}, f32[2,32,8192]{2,1,0:T(8,128)}, u32[]{:S(2)}) copy-start(f32[2,32,8192]{2,1,0:T(8,128)} %param.8) | copy-start | bytes 6291460
  288.2 3.1 copy-start.4
  291.3 20.1 %copy-start.1 = (bf16[1,2,32,8192]{3,2,1,0:T(8,128)(2,1)S(1)}, bf16[1,2,32,8192]{3,2,1,0:T(8,128)(2,1)}, u32[]{:S(2)}) copy-start(bf16[1,2,32,8192]{3,2,1,0:T(8,128)(2,1)} %param.6) | copy-start | bytes 3145732
  291.3 20.1 %copy-start.2 = (bf16[1,2,32,8192]{3,2,1,0:T(8,128)(2,1)S(1)}, bf16[1,2,32,8192]{3,2,1,0:T(8,128)(2,1)}, u32[]{:S(2)}) copy-start(bf16[1,2,32,8192]{3,2,1,0:T(8,128)(2,1)} %param.7) | copy-start | bytes 3145732
Sparse Core Ops, SparseCore 0:
  24.6 263.5 all-reduce.1
where the time goes:
time: 320 us
  waiting for transfers between devices  264 us (82%)
  matrix products  39.6 us (12%)
  between operations  14.1 us (4%)
    psum x1, waiting for transfers between devices, per_device(): total_sketch = lax.psum(partial_sketch, ('rep', 'fsdp')) / replicas  264 us
    dot_general x1, matrix products, per_device(): update = jnp.einsum('mpk,nk->pmn', projected, signed, precision=highest)  20.1 us
    dot_general x1, matrix products, per_device(): jnp.einsum('pmn,nk->mpk', accumulated[0], signed, precision=highest)  14 us
  transfers between devices with their start and end apart: 1, of which 1 were waited for; matrix products, arithmetic and copies ran while one was open for 0% of the time, Pallas kernels for 0%

commit v1 on v0

v1 whole, which is shorter than its diff:
```python
import functools

import jax
import jax.numpy as jnp
from jax import lax
from jax.experimental import pallas as pl
from jax.experimental.pallas import tpu as pltpu
from jax.sharding import Mesh, PartitionSpec as P

K2 = 512
HALF = K2 // 2
PLANE = ("xh", "y", "xl", "c")
SIZES = (("xh", 2), ("y", 4), ("z", 8), ("xl", 2), ("c", 2))
REP = ("xh", "y")
FSDP = ("z", "xl", "c")
CHUNK = 1024
NT = (((1,), (1,)), ((), ()))


def split(x):
    hi = x.astype(jnp.bfloat16)
    lo = (x - hi.astype(jnp.float32)).astype(jnp.bfloat16)
    return hi, lo


def hash_parts(h):
    sign = (1 - 2 * (h >> 9)).astype(jnp.float32)
    upper = ((h >> 8) & 1) == 1
    return h & (HALF - 1), upper, sign


def onehot(low, width):
    rows = lax.broadcasted_iota(jnp.int32, (HALF, width), 0)
    return jnp.where(rows == low, jnp.float32(1), jnp.float32(0)).astype(jnp.bfloat16)


def sketch_kernel(hash_ref, deltas_ref, residual_ref, out_ref, sum_ref):
    step = pl.program_id(0)
    width = hash_ref.shape[1]
    low, upper, sign = hash_parts(hash_ref[...])
    zero = jnp.zeros_like(sign)
    lower_sign = jnp.where(upper, zero, sign).astype(jnp.bfloat16)
    upper_sign = jnp.where(upper, sign, zero).astype(jnp.bfloat16)
    d = deltas_ref[0].reshape(-1, width)
    r = residual_ref[0].reshape(-1, width)
    wide = jnp.concatenate(
        [d * lower_sign, d * upper_sign, r * lower_sign, r * upper_sign], axis=0
    )
    part = lax.dot_general(
        onehot(low, width), wide, NT, preferred_element_type=jnp.float32
    )

    @pl.when(step == 0)
    def _():
        sum_ref[...] = part

    @pl.when(step > 0)
    def _():
        sum_ref[...] += part

    @pl.when(step == pl.num_programs(0) - 1)
    def _():
        z = sum_ref[...]
        n = z.shape[1] // 2
        out_ref[...] = (z[:, :n] + z[:, n:]).reshape(out_ref.shape)


def sketch(deltas, residual, hashes):
    _, p, m, n = deltas.shape
    block = pl.BlockSpec((1, p, m, CHUNK), lambda j: (0, 0, 0, j))
    lanes = 2 * p * m
    return pl.pallas_call(
        sketch_kernel,
        grid=(n // CHUNK,),
        in_specs=[pl.BlockSpec((1, CHUNK), lambda j: (0, j)), block, block],
        out_specs=pl.BlockSpec((32, HALF // 32, lanes), lambda j: (0, 0, 0)),
        out_shape=jax.ShapeDtypeStruct((32, HALF // 32, lanes), jnp.float32),
        scratch_shapes=[pltpu.VMEM((HALF, 2 * lanes), jnp.float32)],
        name="sketch",
    )(hashes, deltas, residual)


def left_wide(ref):
    block = ref[...].astype(jnp.bfloat16)
    return jnp.concatenate([block] * 4, axis=0)


def quarter_mask(rows):
    lane = lax.broadcasted_iota(jnp.int32, (rows, 128), 1)
    row = lax.broadcasted_iota(jnp.int32, (rows, 128), 0)
    return (lane // 32) == (row // (rows // 4))


def reduce_kernel(me_ref, recv_ref, l0, l1, l2, l3, out_ref, sum_ref):
    sum_ref[...] = jnp.sum(recv_ref[...], axis=0)
    me = me_ref[0]
    mask = quarter_mask(32)
    total = jnp.zeros(out_ref.shape, jnp.float32)
    for j, l in enumerate((l0, l1, l2, l3)):
        y = sum_ref[me ^ j]
        y = jnp.where(mask, jnp.concatenate([y] * 4, axis=0), 0.0)
        both = jnp.concatenate(split(y), axis=0)
        t = jnp.dot(both, left_wide(l), preferred_element_type=jnp.float32)
        total += t[:32] + t[32:]
    out_ref[...] = total


def reduce_columns(me, recv, lefts):
    vmem = pl.BlockSpec(memory_space=pltpu.VMEM)
    return pl.pallas_call(
        reduce_kernel,
        in_specs=[pl.BlockSpec(memory_space=pltpu.SMEM)] + [vmem] * 5,
        out_specs=vmem,
        out_shape=jax.ShapeDtypeStruct((32, lefts[0].shape[1]), jnp.float32),
        scratch_shapes=[pltpu.VMEM((4, 8, 128), jnp.float32)],
        name="reduce_columns",
    )(me, recv, *lefts)


def expand_kernel(terms, replicas, me_ref, *refs):
    parts, lefts, out_ref = refs[:terms], refs[terms : terms + 4], refs[terms + 4]
    me = me_ref[0]
    mask = quarter_mask(32)
    c = parts[0][...]
    for part in parts[1:]:
        c = c + part[...]
    both = jnp.concatenate(split(c / replicas), axis=0)
    for j, l in enumerate(lefts):
        t = lax.dot_general(
            both, left_wide(l), NT, preferred_element_type=jnp.float32
        )
        t = jnp.where(mask, t[:32] + t[32:], 0.0)
        t = t[0:8] + t[8:16] + t[16:24] + t[24:32]
        for rep in range(out_ref.shape[0]):
            out_ref[rep, me ^ j] = t


def expand_columns(me, parts, lefts, replicas):
    vmem = pl.BlockSpec(memory_space=pltpu.VMEM)
    return pl.pallas_call(
        functools.partial(expand_kernel, len(parts), replicas),
        in_specs=[pl.BlockSpec(memory_space=pltpu.SMEM)] + [vmem] * (len(parts) + 4),
        out_specs=vmem,
        out_shape=jax.ShapeDtypeStruct((8, 4, 8, 128), jnp.float32),
        name="expand_columns",
    )(me, *parts, *lefts)


def apply_kernel(
    hash_ref, p_ref, deltas_ref, residual_ref, params_ref, momentum_ref,
    new_params_ref, new_momentum_ref, new_residual_ref, left_ref,
):
    @pl.when(pl.program_id(0) == 0)
    def _():
        hi, lo = split(p_ref[...].T)
        left_ref[: hi.shape[0]] = hi
        left_ref[hi.shape[0] :] = lo

    width = hash_ref.shape[1]
    low, upper, sign = hash_parts(hash_ref[...])
    both = jnp.dot(
        left_ref[...], onehot(low, width), preferred_element_type=jnp.float32
    )
    rows = both.shape[0] // 4
    both = both[: 2 * rows] + both[2 * rows :]
    u = jnp.where(upper, both[rows:], both[:rows]) * sign
    u = u.reshape(params_ref.shape)
    acc = residual_ref[0].astype(jnp.float32) + deltas_ref[0].astype(jnp.float32)
    new_residual_ref[0] = (acc - u).astype(jnp.bfloat16)
    new_momentum = 0.9 * momentum_ref[...] + u
    new_momentum_ref[...] = new_momentum
    new_params_ref[...] = params_ref[...] - 0.7 * (u + 0.9 * new_momentum)


def apply_update(hashes, projected, deltas, residual, params, momentum):
    p, m, n = params.shape
    wide = pl.BlockSpec((p, m, CHUNK), lambda j: (0, 0, j))
    narrow = pl.BlockSpec((1, p, m, CHUNK), lambda j: (0, 0, 0, j))
    return pl.pallas_call(
        apply_kernel,
        grid=(n // CHUNK,),
        in_specs=[
            pl.BlockSpec((1, CHUNK), lambda j: (0, j)),
            pl.BlockSpec(projected.shape, lambda j: (0, 0)),
            narrow, narrow, wide, wide,
        ],
        out_specs=[wide, wide, narrow],
        out_shape=[
            jax.ShapeDtypeStruct(params.shape, jnp.float32),
            jax.ShapeDtypeStruct(momentum.shape, jnp.float32),
            jax.ShapeDtypeStruct(residual.shape, jnp.bfloat16),
        ],
        scratch_shapes=[pltpu.VMEM((4 * p * m, HALF), jnp.bfloat16)],
        name="apply_update",
    )(hashes, projected, deltas, residual, params, momentum)


def shifted(x, by):
    return lax.ppermute(x, "z", [(i, (i + by) % 8) for i in range(8)])


def sum_over_z(x):
    right = shifted(x, 1)
    left = shifted(x, -1)
    pair = x + right
    triple = pair + left
    return triple, shifted(triple, -3), shifted(pair, 2)


def per_device(deltas, residual, params, momentum, left_sketch, right_hash):
    replicas = 1
    for axis in REP:
        replicas *= lax.axis_size(axis)
    me = (lax.axis_index("xl") * 2 + lax.axis_index("c")).astype(jnp.int32).reshape(1)
    left = left_sketch.astype(jnp.float32)
    lefts = [left]
    for j in range(1, 4):
        lefts.append(lax.ppermute(left, ("xl", "c"), [(i, i ^ j) for i in range(4)]))
    hashes = right_hash.reshape(1, -1)
    sent = sketch(deltas, residual, hashes)
    recv = lax.all_to_all(sent, PLANE, 0, 0).reshape(8, 4, 8, 128)
    parts = sum_over_z(reduce_columns(me, recv, lefts))
    back = expand_columns(me, parts, lefts, replicas).reshape(32, 8, 128)
    projected = lax.all_to_all(back, PLANE, 0, 0).reshape(HALF, 128)
    return tuple(
        apply_update(hashes, projected, deltas, residual, params, momentum)
    )


def solution(mesh):
    names, sizes = zip(*SIZES)
    fine = Mesh(mesh.devices.reshape(sizes), names)
    rows = P(None, FSDP, None)
    tall = P(REP, None, FSDP, None)
    return jax.shard_map(
        per_device,
        mesh=fine,
        in_specs=(tall, tall, rows, rows, P(FSDP, None), P()),
        out_specs=(rows, rows, tall),
        check_vma=False,
    )
```

time: 320 us -> 71.9 us (0.22)
  waiting for transfers between devices: 264 us -> 13.4 us
  matrix products: 39.6 us -> 0 us
  Pallas kernels: 0 us -> 19.7 us
  starting transfers between devices: 0.04 us -> 18.5 us
  blocking collectives: 0 us -> 16.7 us
  between operations: 14.1 us -> 0.71 us
    psum x1 -> x0, waiting for transfers between devices: 264 us -> none  [per_device(): total_sketch = lax.psum(partial_sketch, ('rep', 'fsdp')) / replicas]
    dot_general x4 -> x0, matrix products: 39.6 us -> none  [the longest x1 20.1 us: per_device(): update = jnp.einsum('mpk,nk->pmn', projected, signed, precision=highest)]
    pallas_call x0 -> x4, Pallas kernels: none -> 19.7 us  [the longest x1 9.23 us: apply_update(): pl.pallas_call(apply_kernel, grid=(n // CHUNK,), in_specs=[pl.BlockSpec((...]
    all_to_all x0 -> x1, blocking collectives: none -> 16.7 us  [per_device(): projected = lax.all_to_all(back, PLANE, 0, 0).reshape(HALF, 128)]
    ppermute x0 -> x7, waiting for transfers between devices: none -> 12.5 us  [the longest x4 8.26 us: shifted(): return lax.ppermute(x, 'z', [(i, (i + by) % 8) for i in range(8)])]
    ppermute x0 -> x7, starting transfers between devices: none -> 9.97 us  [the longest x4 7.74 us: shifted(): return lax.ppermute(x, 'z', [(i, (i + by) % 8) for i in range(8)])]
    all_to_all x0 -> x1, starting transfers between devices: none -> 8.58 us  [per_device(): recv = lax.all_to_all(sent, PLANE, 0, 0).reshape(8, 4, 8, 128)]
  transfers between devices with their start and end apart: 1 -> 8, of which waited for: 1 -> 7; matrix products, arithmetic and copies ran while one was open for 0% -> 0% of each run, Pallas kernels for 0% -> 0%
where the time goes in v1:
time: 71.9 us; the launch traced here: 71.3 us
  Pallas kernels  19.7 us (27%)
  starting transfers between devices  18.5 us (26%)
  blocking collectives  16.7 us (23%)
  waiting for transfers between devices  13.4 us (19%)
  local copies, waits for them, and re-layouts  1.36 us (2%)
  other arithmetic  0.86 us (1%)
    all_to_all x1, blocking collectives, per_device(): projected = lax.all_to_all(back, PLANE, 0, 0).reshape(HALF, 128)  16.7 us
    pallas_call x1, Pallas kernels, apply_update(): pl.pallas_call(apply_kernel, grid=(n // CHUNK,), in_specs=[pl.BlockSpec((...  9.23 us
    all_to_all x1, starting transfers between devices, per_device(): recv = lax.all_to_all(sent, PLANE, 0, 0).reshape(8, 4, 8, 128)  8.58 us
    ppermute x4, waiting for transfers between devices, shifted(): return lax.ppermute(x, 'z', [(i, (i + by) % 8) for i in range(8)])  8.26 us
    ppermute x4, starting transfers between devices, shifted(): return lax.ppermute(x, 'z', [(i, (i + by) % 8) for i in range(8)])  7.74 us
    pallas_call x1, Pallas kernels, sketch(): pl.pallas_call(sketch_kernel, grid=(n // CHUNK,), in_specs=[pl.BlockSpec(...  6.62 us
    ppermute x3, waiting for transfers between devices, per_device(): lax.ppermute(left, ('xl', 'c'), [(i, i ^ j) for i in range(4)])  4.19 us
    ppermute x3, starting transfers between devices, per_device(): lax.ppermute(left, ('xl', 'c'), [(i, i ^ j) for i in range(4)])  2.23 us
  transfers between devices with their start and end apart: 8, of which 7 were waited for; matrix products, arithmetic and copies ran while one was open for 0% of the time, Pallas kernels for 0%

profile of v1, /device:TPU:1, one launch (start us, length us, event | category | flops | bytes accessed | tf_op | source)
XLA Modules:
  0.0 71.3 jit_solution(7367971796993802206)
XLA Ops:
  0.6 0.0 copy-start.8
  0.6 6.6 %sketch.1 = f32[32,8,128]{2,1,0:T(8,128)} custom-call(s32[1,8192]{1,0:T(1,128)} %bitcast.8, bf16[1,2,32,8192]{3,2,1,0:T(8,128)(2,1)} %deltas_ref.3, bf16[1,2,32,8192]{3,2,1,0:T(8,128)(2,1)} %residual_ref.3), custom_call_target="tpu_custom_call" | custom-call | tf_op jit(solution)/shard_map/sketch/pallas_call | solution.py:72
  7.3 8.6 %all-to-all-start = ((f32[32,8,128]{2,1,0:T(8,128)}), f32[32,8,128]{2,1,0:T(8,128)S(1)}, u32[]{:S(2)}, u32[]{:S(2)}) async-start(f32[32,8,128]{2,1,0:T(8,128)} %sketch.1), calls=%async_computation | async-start | bytes 262144 | tf_op jit(solution)/shard_map/all_to_all | solution.py:221
  15.8 0.0 copy-done.8
  15.9 0.0 copy-start
  15.9 1.7 %collective-permute-start.2 = (f32[32,512]{1,0:T(8,128)S(1)}, f32[32,512]{1,0:T(8,128)S(1)}, u32[]{:S(2)}, u32[]{:S(2)}) collective-permute-start(f32[32,512]{1,0:T(8,128)S(1)} %convert_element_type.3.l0.refs_3_), channel_id=1, source_target_pairs={{0,3},{1,2},{2,1},{3,0},{4,7},{5,6},{6,5},{7,4},{8,11},{9,10},{10,... | collective-permute-start | bytes 196616 | tf_op jit(solution)/shard_map/ppermute | solution.py:218
  17.6 0.0 collective-permute-start.1
  17.6 0.5 collective-permute-start
  18.1 3.7 %collective-permute-done.2.l3.refs_6_ = f32[32,512]{1,0:T(8,128)S(1)} collective-permute-done((f32[32,512]{1,0:T(8,128)S(1)}, f32[32,512]{1,0:T(8,128)S(1)}, u32[]{:S(2)}, u32[]{:S(2)}) %collective-permute-start.2) | collective-permute-done | bytes 65568 | tf_op jit(solution)/shard_map/ppermute | solution.py:218
  21.9 0.5 collective-permute-done.1.l2.refs_5_
  22.3 0.0 collective-permute-done.l1.refs_4_
  22.3 1.0 %all-to-all-done = f32[32,8,128]{2,1,0:T(8,128)S(1)} async-done(((f32[32,8,128]{2,1,0:T(8,128)}), f32[32,8,128]{2,1,0:T(8,128)S(1)}, u32[]{:S(2)}, u32[]{:S(2)}) %all-to-all-start) | async-done | bytes 131104 | tf_op jit(solution)/shard_map/all_to_all | solution.py:221
  23.3 0.0 copy-done
  23.3 0.0 copy-done.3
  23.3 0.0 copy-done.4
  23.3 0.0 copy-done.5
  23.3 0.6 copy-done.1
  24.0 1.9 %reduce_columns.1 = f32[32,512]{1,0:T(8,128)} custom-call(s32[1]{0:T(128)} %bitcast.1.me_ref, f32[8,4,8,128]{3,2,1,0:T(8,128)} %bitcast.6, f32[32,512]{1,0:T(8,128)} %copy-done, f32[32,512]{1,0:T(8,128)} %copy-done.5, f32[32,512]{1,0:T(8,128)} %copy-done.4, f32[32,512]{1,0:T(8,128)} %copy-done.3), custom_call_target="tpu_custom_call" | custom-call | tf_op jit(solution)/shard_map/reduce_columns/pallas_call | solution.py:110
  25.8 5.6 %collective-permute-start.4 = (f32[32,512]{1,0:T(8,128)}, f32[32,512]{1,0:T(8,128)S(1)}, u32[]{:S(2)}, u32[]{:S(2)}) collective-permute-start(f32[32,512]{1,0:T(8,128)} %reduce_columns.1), channel_id=1, source_target_pairs={{0,28},{4,0},{8,4},{12,8},{16,12},{20,16},{24,20},{28,24},{1,29},{... | collective-permute-start | bytes 196616 | tf_op jit(solution)/shard_map/ppermute | solution.py:199
  31.4 0.0 collective-permute-start.3
  31.4 1.6 %collective-permute-done.4 = f32[32,512]{1,0:T(8,128)S(1)} collective-permute-done((f32[32,512]{1,0:T(8,128)}, f32[32,512]{1,0:T(8,128)S(1)}, u32[]{:S(2)}, u32[]{:S(2)}) %collective-permute-start.4) | collective-permute-done | bytes 65568 | tf_op jit(solution)/shard_map/ppermute | solution.py:199
  33.0 2.9 %collective-permute-done.3 = f32[32,512]{1,0:T(8,128)S(1)} collective-permute-done((f32[32,512]{1,0:T(8,128)}, f32[32,512]{1,0:T(8,128)S(1)}, u32[]{:S(2)}, u32[]{:S(2)}) %collective-permute-start.3) | collective-permute-done | bytes 65568 | tf_op jit(solution)/shard_map/ppermute | solution.py:199
  35.9 0.9 %fusion = (f32[32,512]{1,0:T(8,128)S(1)}, f32[32,512]{1,0:T(8,128)S(1)}) fusion(f32[32,512]{1,0:T(8,128)S(1)} %collective-permute-done.4, f32[32,512]{1,0:T(8,128)} %reduce_columns.1, f32[32,512]{1,0:T(8,128)S(1)} %collective-permute-done.3), kind=kLoop, calls=%fused_computation | loop fusion | flops 32768 | bytes 327680 | tf_op jit(solution)/shard_map/add | solution.py:206
  36.8 0.1 collective-permute-start.6
  36.9 2.1 %collective-permute-start.5 = (f32[32,512]{1,0:T(8,128)S(1)}, f32[32,512]{1,0:T(8,128)S(1)}, u32[]{:S(2)}, u32[]{:S(2)}) collective-permute-start(f32[32,512]{1,0:T(8,128)S(1)} %get-tuple-element.3.refs_0_), channel_id=1, source_target_pairs={{0,20},{4,24},{8,28},{12,0},{16,4},{20,8},{24,12},{28,16},{1,21},{... | collective-permute-start | bytes 196616 | tf_op jit(solution)/shard_map/ppermute | solution.py:199
  39.0 3.2 %collective-permute-done.6.refs_2_ = f32[32,512]{1,0:T(8,128)S(1)} collective-permute-done((f32[32,512]{1,0:T(8,128)S(1)}, f32[32,512]{1,0:T(8,128)S(1)}, u32[]{:S(2)}, u32[]{:S(2)}) %collective-permute-start.6) | collective-permute-done | bytes 65568 | tf_op jit(solution)/shard_map/ppermute | solution.py:199
  42.2 0.5 collective-permute-done.5.refs_1_
  42.7 0.1 copy-done.6
  42.8 0.6 copy-done.7
  43.4 2.0 %expand_columns.1 = f32[8,4,8,128]{3,2,1,0:T(8,128)} custom-call(s32[1]{0:T(128)} %bitcast.1.me_ref, f32[32,512]{1,0:T(8,128)} %copy-done.2, f32[32,512]{1,0:T(8,128)} %copy-done.7, f32[32,512]{1,0:T(8,128)} %copy-done.6, f32[32,512]{1,0:T(8,128)} %copy-done, f32[32,512]{1,0:T(8,128)} %copy-done.5, f32[32,512]{1,0:T(8,128)} %copy-done.4, f32[32,512]{1,0:T(8,128)} %copy-done.3), custom_call_target="tpu_custom_call" | custom-call | tf_op jit(solution)/shard_map/expand_columns/pallas_call | solution.py:140
  45.4 16.7 %all_to_all.10 = f32[32,8,128]{2,1,0:T(8,128)} all-to-all(f32[32,8,128]{2,1,0:T(8,128)} %bitcast.7), channel_id=1, replica_groups=mesh['xh'=2,'y'=4,'z'=8,'xl'=2,'c'=2] {'xh','y','xl','c'}, dimensions={0} | all-to-all | bytes 262144 | tf_op jit(solution)/shard_map/all_to_all | solution.py:224
  62.1 9.2 %apply_update.1 = (f32[2,32,8192]{2,1,0:T(8,128)}, f32[2,32,8192]{2,1,0:T(8,128)}, bf16[1,2,32,8192]{3,2,1,0:T(8,128)(2,1)}) custom-call(s32[1,8192]{1,0:T(1,128)} %bitcast.9, f32[256,128]{1,0:T(8,128)} %bitcast.5, bf16[1,2,32,8192]{3,2,1,0:T(8,128)(2,1)} %deltas_ref.3, bf16[1,2,32,8192]{3,2,1,0:T(8,128)(2,1)} %residual_ref.3, f32[2,32,8192]{2,1,0:T(8,128)} %params_ref.1, ...), custom_call_target="tpu_custom_call" | custom-call | tf_op jit(solution)/shard_map/apply_update/pallas_call | solution.py:179
  (9 shorter events, 0.0 us)
Async XLA Ops:
  0.6 15.2 %copy-start.8 = (bf16[32,512]{1,0:T(8,128)(2,1)S(1)}, bf16[32,512]{1,0:T(8,128)(2,1)}, u32[]{:S(2)}) copy-start(bf16[32,512]{1,0:T(8,128)(2,1)} %param.10) | copy-start | bytes 98308
  7.3 16.1 %all-to-all-start = ((f32[32,8,128]{2,1,0:T(8,128)}), f32[32,8,128]{2,1,0:T(8,128)S(1)}, u32[]{:S(2)}, u32[]{:S(2)}) async-start(f32[32,8,128]{2,1,0:T(8,128)} %sketch.1), calls=%async_computation | async-start | bytes 262144 | tf_op jit(solution)/shard_map/all_to_all | solution.py:221
  15.9 7.4 %copy-start = (f32[32,512]{1,0:T(8,128)}, f32[32,512]{1,0:T(8,128)S(1)}, u32[]{:S(2)}) copy-start(f32[32,512]{1,0:T(8,128)S(1)} %convert_element_type.3.l0.refs_3_) | copy-start | bytes 196612
  15.9 6.0 %collective-permute-start.2 = (f32[32,512]{1,0:T(8,128)S(1)}, f32[32,512]{1,0:T(8,128)S(1)}, u32[]{:S(2)}, u32[]{:S(2)}) collective-permute-start(f32[32,512]{1,0:T(8,128)S(1)} %convert_element_type.3.l0.refs_3_), channel_id=1, source_target_pairs={{0,3},{1,2},{2,1},{3,0},{4,7},{5,6},{6,5},{7,4},{8,11},{9,10},{10,... | collective-permute-start | bytes 196616 | tf_op jit(solution)/shard_map/ppermute | solution.py:218
  17.6 4.7 %collective-permute-start.1 = (f32[32,512]{1,0:T(8,128)S(1)}, f32[32,512]{1,0:T(8,128)S(1)}, u32[]{:S(2)}, u32[]{:S(2)}) collective-permute-start(f32[32,512]{1,0:T(8,128)S(1)} %convert_element_type.3.l0.refs_3_), channel_id=1, source_target_pairs={{0,2},{1,3},{2,0},{3,1},{4,6},{5,7},{6,4},{7,5},{8,10},{9,11},{10,... | collective-permute-start | bytes 196616 | tf_op jit(solution)/shard_map/ppermute | solution.py:218
  17.6 4.7 %collective-permute-start = (f32[32,512]{1,0:T(8,128)S(1)}, f32[32,512]{1,0:T(8,128)S(1)}, u32[]{:S(2)}, u32[]{:S(2)}) collective-permute-start(f32[32,512]{1,0:T(8,128)S(1)} %convert_element_type.3.l0.refs_3_), channel_id=1, source_target_pairs={{0,1},{1,0},{2,3},{3,2},{4,5},{5,4},{6,7},{7,6},{8,9},{9,8},{10,11... | collective-permute-start | bytes 196616 | tf_op jit(solution)/shard_map/ppermute | solution.py:218
  21.9 1.5 %copy-start.3 = (f32[32,512]{1,0:T(8,128)}, f32[32,512]{1,0:T(8,128)S(1)}, u32[]{:S(2)}) copy-start(f32[32,512]{1,0:T(8,128)S(1)} %collective-permute-done.2.l3.refs_6_) | copy-start | bytes 196612
  22.3 1.0 %copy-start.4 = (f32[32,512]{1,0:T(8,128)}, f32[32,512]{1,0:T(8,128)S(1)}, u32[]{:S(2)}) copy-start(f32[32,512]{1,0:T(8,128)S(1)} %collective-permute-done.1.l2.refs_5_) | copy-start | bytes 196612
  22.3 1.0 %copy-start.5 = (f32[32,512]{1,0:T(8,128)}, f32[32,512]{1,0:T(8,128)S(1)}, u32[]{:S(2)}) copy-start(f32[32,512]{1,0:T(8,128)S(1)} %collective-permute-done.l1.refs_4_) | copy-start | bytes 196612
  23.3 0.7 copy-start.1
  25.8 7.2 %collective-permute-start.4 = (f32[32,512]{1,0:T(8,128)}, f32[32,512]{1,0:T(8,128)S(1)}, u32[]{:S(2)}, u32[]{:S(2)}) collective-permute-start(f32[32,512]{1,0:T(8,128)} %reduce_columns.1), channel_id=1, source_target_pairs={{0,28},{4,0},{8,4},{12,8},{16,12},{20,16},{24,20},{28,24},{1,29},{... | collective-permute-start | bytes 196616 | tf_op jit(solution)/shard_map/ppermute | solution.py:199
  31.4 4.5 %collective-permute-start.3 = (f32[32,512]{1,0:T(8,128)}, f32[32,512]{1,0:T(8,128)S(1)}, u32[]{:S(2)}, u32[]{:S(2)}) collective-permute-start(f32[32,512]{1,0:T(8,128)} %reduce_columns.1), channel_id=1, source_target_pairs={{0,4},{4,8},{8,12},{12,16},{16,20},{20,24},{24,28},{28,0},{1,5},{5... | collective-permute-start | bytes 196616 | tf_op jit(solution)/shard_map/ppermute | solution.py:199
  36.8 5.9 %copy-start.2 = (f32[32,512]{1,0:T(8,128)}, f32[32,512]{1,0:T(8,128)S(1)}, u32[]{:S(2)}) copy-start(f32[32,512]{1,0:T(8,128)S(1)} %get-tuple-element.3.refs_0_) | copy-start | bytes 196612
  36.8 5.3 %collective-permute-start.6 = (f32[32,512]{1,0:T(8,128)S(1)}, f32[32,512]{1,0:T(8,128)S(1)}, u32[]{:S(2)}, u32[]{:S(2)}) collective-permute-start(f32[32,512]{1,0:T(8,128)S(1)} %get-tuple-element.4), channel_id=1, source_target_pairs={{0,8},{4,12},{8,16},{12,20},{16,24},{20,28},{24,0},{28,4},{1,9},{5... | collective-permute-start | bytes 196616 | tf_op jit(solution)/shard_map/ppermute | solution.py:199
  36.9 5.8 %collective-permute-start.5 = (f32[32,512]{1,0:T(8,128)S(1)}, f32[32,512]{1,0:T(8,128)S(1)}, u32[]{:S(2)}, u32[]{:S(2)}) collective-permute-start(f32[32,512]{1,0:T(8,128)S(1)} %get-tuple-element.3.refs_0_), channel_id=1, source_target_pairs={{0,20},{4,24},{8,28},{12,0},{16,4},{20,8},{24,12},{28,16},{1,21},{... | collective-permute-start | bytes 196616 | tf_op jit(solution)/shard_map/ppermute | solution.py:199
  42.2 0.6 copy-start.6
  42.8 0.6 copy-start.7

commit v2 on v0

v2 whole, which is shorter than its diff:
```python
import functools

import jax
import jax.numpy as jnp
import numpy as np
from jax import lax
from jax.experimental import pallas as pl
from jax.experimental.pallas import tpu as pltpu
from jax.sharding import Mesh, PartitionSpec as P

K2 = 512
HALF = K2 // 2
PAIR = 1
LEFT_FORM = 'gather'
SUM_FORM = "double"
RINGS = 8 // PAIR
SIZES = (("xh", 2), ("y", 4), ("zh", RINGS), ("z0", PAIR), ("xl", 2), ("c", 2))
REP = ("xh", "y")
FSDP = ("zh", "z0", "xl", "c")
NEAR = ("z0", "xl", "c")
GROUP = REP + NEAR
ROW_SETS = 4 * PAIR
BLOCKS = 8 * ROW_SETS
KEPT = HALF // BLOCKS
LEFT_TILES = 2
CHUNK = 2048
NT = (((1,), (1,)), ((), ()))
VMEM_BLOCK = pl.BlockSpec(memory_space=pltpu.VMEM)
HBM_BLOCK = pl.BlockSpec(memory_space=pltpu.HBM)
SMEM_BLOCK = pl.BlockSpec(memory_space=pltpu.SMEM)
PARAMS = pltpu.CompilerParams(vmem_limit_bytes=24 * 2**20)
SMALL = pltpu.CompilerParams(vmem_limit_bytes=8 * 2**20)


def in_vmem(x):
    return pltpu.with_memory_space_constraint(x, pltpu.VMEM)


def in_hbm(x):
    return pltpu.with_memory_space_constraint(x, pltpu.HBM)


def split(x):
    hi = x.astype(jnp.bfloat16)
    lo = (x - hi.astype(jnp.float32)).astype(jnp.bfloat16)
    return jnp.concatenate([hi, lo], axis=0)


def hash_parts(h):
    sign = (1 - 2 * (h >> 9)).astype(jnp.float32)
    upper = ((h >> 8) & 1) == 1
    return h & (HALF - 1), upper, sign


def onehot(low, width):
    rows = lax.broadcasted_iota(jnp.int16, (HALF, width), 0)
    return jnp.where(rows == low.astype(jnp.int16), jnp.bfloat16(1), jnp.bfloat16(0))


def sketch_kernel(
    rank_ref, hash_in, deltas_in, residual_in, left_in, out_ref,
    hash_ref, deltas_ref, residual_ref, left_ref, wide_ref, sems,
):
    pairs = (
        (hash_in, hash_ref), (left_in, left_ref),
        (deltas_in, deltas_ref), (residual_in, residual_ref),
    )
    copies = [
        pltpu.make_async_copy(there, here, sems.at[i])
        for i, (there, here) in enumerate(pairs)
    ]
    for copy in copies:
        copy.start()
    copies[0].wait()
    copies[1].wait()
    rank = rank_ref[0]
    wide_ref[...] = left_ref[...].astype(jnp.float32)
    rows = wide_ref[pl.ds(pl.multiple_of((rank >> 1) * 8, 8), 8), :]
    half = rows.shape[1] // 2
    rows = jnp.where((rank & 1) == 1, rows[:, half:], rows[:, :half])
    for i in range(LEFT_TILES):
        tile = rows[:, i * 128 : (i + 1) * 128]
        out_ref[:, (i + 1) * KEPT : (i + 2) * KEPT, :] = jnp.broadcast_to(
            tile[None], (BLOCKS,) + tile.shape
        )
    width = hash_ref.shape[1]
    low, upper, sign = hash_parts(hash_ref[...])
    zero = jnp.zeros_like(sign)
    lower_sign = jnp.where(upper, zero, sign).astype(jnp.bfloat16)
    upper_sign = jnp.where(upper, sign, zero).astype(jnp.bfloat16)
    copies[2].wait()
    copies[3].wait()
    d = deltas_ref[0].reshape(-1, width)
    r = residual_ref[0].reshape(-1, width)
    wide = jnp.concatenate(
        [d * lower_sign, d * upper_sign, r * lower_sign, r * upper_sign], axis=0
    )
    z = lax.dot_general(
        onehot(low, width), wide, NT, preferred_element_type=jnp.float32
    )
    n = z.shape[1] // 2
    out_ref[:, :KEPT, :] = (z[:, :n] + z[:, n:]).reshape(BLOCKS, KEPT, n)


def sketch(rank, hashes, deltas, residual, left):
    _, p, m, _ = deltas.shape
    arrays = (hashes, deltas, residual, left)
    return pl.pallas_call(
        sketch_kernel,
        in_specs=[SMEM_BLOCK] + [HBM_BLOCK] * 4,
        out_specs=VMEM_BLOCK,
        out_shape=pltpu.VMEM((BLOCKS, (1 + LEFT_TILES) * KEPT, 2 * p * m), jnp.float32),
        scratch_shapes=[
            *[pltpu.VMEM(x.shape, x.dtype) for x in arrays],
            pltpu.VMEM(left.shape, jnp.float32),
            pltpu.SemaphoreType.DMA((4,)),
        ],
        compiler_params=PARAMS,
        name="sketch",
    )(rank, *map(in_hbm, arrays))


def quarter_mask(rows):
    lane = lax.broadcasted_iota(jnp.int32, (rows, 128), 1)
    row = lax.broadcasted_iota(jnp.int32, (rows, 128), 0)
    return (lane // 32) == (row // (rows // 4))


def reduce_kernel(recv_ref, out_ref, left_ref):
    mask = quarter_mask(4 * KEPT)
    wide = []
    for f in range(ROW_SETS):
        rows = []
        for i in range(0, 8, 2):
            tiles = [
                recv_ref[i + j, f, (t + 1) * KEPT : (t + 2) * KEPT, :]
                for j in range(2)
                for t in range(LEFT_TILES)
            ]
            rows.append(jnp.concatenate(tiles, axis=1))
        rows = jnp.concatenate(rows, axis=0).astype(jnp.bfloat16)
        for q in range(4):
            at = (4 * f + q) * rows.shape[0]
            left_ref[at : at + rows.shape[0]] = rows
        part = jnp.sum(recv_ref[:, f, :KEPT, :], axis=0)
        wide.append(jnp.where(mask, jnp.concatenate([part] * 4, axis=0), 0.0))
    wide = split(jnp.concatenate(wide, axis=1))
    t = jnp.dot(wide, left_ref[...], preferred_element_type=jnp.float32)
    out_ref[...] = t[: 4 * KEPT] + t[4 * KEPT :]


def reduce_columns(recv, width):
    return pl.pallas_call(
        reduce_kernel,
        in_specs=[VMEM_BLOCK],
        out_specs=[VMEM_BLOCK] * 2,
        out_shape=[
            pltpu.VMEM((4 * KEPT, width), jnp.float32),
            pltpu.VMEM((128 * ROW_SETS, width), jnp.bfloat16),
        ],
        compiler_params=SMALL,
        name="reduce_columns",
    )(in_vmem(recv))


def expand_kernel(terms, replicas, *refs):
    parts, left_ref, out_ref = refs[:terms], refs[terms], refs[terms + 1]
    mask = quarter_mask(4 * KEPT)
    c = parts[0][...]
    for part in parts[1:]:
        c = c + part[...]
    wide = lax.dot_general(
        split(c / replicas), left_ref[...], NT, preferred_element_type=jnp.float32
    )
    wide = wide[: 4 * KEPT] + wide[4 * KEPT :]
    rows = []
    for f in range(ROW_SETS):
        t = jnp.where(mask, wide[:, f * 128 : (f + 1) * 128], 0.0)
        t = t[: 2 * KEPT] + t[2 * KEPT :]
        rows.append(t[:KEPT] + t[KEPT:])
    rows = jnp.concatenate(rows, axis=0)
    for rep in range(8):
        out_ref[rep * rows.shape[0] : (rep + 1) * rows.shape[0]] = rows


def expand_columns(parts, left, replicas):
    return pl.pallas_call(
        functools.partial(expand_kernel, len(parts), replicas),
        in_specs=[VMEM_BLOCK] * (len(parts) + 1),
        out_specs=VMEM_BLOCK,
        out_shape=pltpu.VMEM((HALF, 128), jnp.float32),
        compiler_params=SMALL,
        name="expand_columns",
    )(*[in_vmem(x) for x in (*parts, left)])


def apply_kernel(
    hash_ref, p_ref, deltas_in, residual_in, momentum_in, params_in,
    params_out, momentum_out, residual_out,
    deltas_ref, residual_ref, momentum_ref, params_ref,
    new_params_ref, new_momentum_ref, new_residual_ref, in_sems, out_sems,
):
    count = hash_ref.shape[1] // CHUNK

    def cut(ref, j):
        return ref.at[(slice(None),) * (len(ref.shape) - 1) + (pl.ds(j * CHUNK, CHUNK),)]

    pairs = (
        (deltas_in, deltas_ref), (residual_in, residual_ref),
        (momentum_in, momentum_ref), (params_in, params_ref),
    )
    loads = [
        [
            pltpu.make_async_copy(cut(there, j), cut(here, j), in_sems.at[i, j])
            for i, (there, here) in enumerate(pairs)
        ]
        for j in range(count)
    ]
    for group in loads:
        for copy in group:
            copy.start()
    left = split(p_ref[...].T)
    rows = left.shape[0] // 4
    stores = []
    for j in range(count):
        at = pl.ds(j * CHUNK, CHUNK)
        low, upper, sign = hash_parts(hash_ref[:, at])
        both = jnp.dot(left, onehot(low, CHUNK), preferred_element_type=jnp.float32)
        both = both[: 2 * rows] + both[2 * rows :]
        u = jnp.where(upper, both[rows:], both[:rows]) * sign
        u = u.reshape(params_ref.shape[:2] + (CHUNK,))
        for copy in loads[j]:
            copy.wait()
        d = deltas_ref[0, :, :, at].astype(jnp.float32)
        acc = residual_ref[0, :, :, at].astype(jnp.float32) + d
        new_residual_ref[0, :, :, at] = (acc - u).astype(jnp.bfloat16)
        new_momentum = 0.9 * momentum_ref[:, :, at] + u
        new_momentum_ref[:, :, at] = new_momentum
        new_params_ref[:, :, at] = params_ref[:, :, at] - 0.7 * (u + 0.9 * new_momentum)
        pairs = (
            (new_residual_ref, residual_out),
            (new_momentum_ref, momentum_out),
            (new_params_ref, params_out),
        )
        for i, (here, there) in enumerate(pairs):
            copy = pltpu.make_async_copy(cut(here, j), cut(there, j), out_sems.at[i, j])
            copy.start()
            stores.append(copy)
    for copy in stores:
        copy.wait()


def apply_update(hashes, projected, deltas, residual, momentum, params):
    wide, narrow = pltpu.VMEM(params.shape, params.dtype), pltpu.VMEM(deltas.shape, deltas.dtype)
    count = params.shape[2] // CHUNK
    return pl.pallas_call(
        apply_kernel,
        in_specs=[VMEM_BLOCK] * 2 + [HBM_BLOCK] * 4,
        out_specs=[HBM_BLOCK] * 3,
        out_shape=[
            jax.ShapeDtypeStruct(params.shape, jnp.float32),
            jax.ShapeDtypeStruct(momentum.shape, jnp.float32),
            jax.ShapeDtypeStruct(residual.shape, jnp.bfloat16),
        ],
        scratch_shapes=[
            narrow, narrow, wide, wide, wide, wide, narrow,
            pltpu.SemaphoreType.DMA((4, count)),
            pltpu.SemaphoreType.DMA((3, count)),
        ],
        compiler_params=PARAMS,
        name="apply_update",
    )(
        in_vmem(hashes), in_vmem(projected),
        *[in_hbm(x) for x in (deltas, residual, momentum, params)],
    )


def sum_over_rings(x):
    swap = lambda v, pairs: lax.ppermute(v, "zh", list(enumerate(pairs)))
    if RINGS == 8:
        x = x + swap(x, [1, 0, 3, 2, 5, 4, 7, 6])
        x = x + swap(x, [2, 3, 0, 1, 6, 7, 4, 5])
        return x, swap(x, [6, 7, 4, 5, 2, 3, 0, 1])
    x = x + swap(x, [1, 0, 3, 2])
    return x, swap(x, [3, 2, 1, 0])


AXES = tuple(name for name, _ in SIZES)
FLIP = True


def plane_groups():
    ids = np.arange(256).reshape([size for _, size in SIZES])
    if FLIP:
        ids = np.roll(ids, (1, 2, 1), (0, 1, 5))
    ids = np.moveaxis(ids, 2, 0).reshape(RINGS, -1)
    return ids.tolist()


def exchange(x):
    return lax.all_to_all(x, AXES, 0, 0, axis_index_groups=plane_groups())


def per_device(deltas, residual, params, momentum, left_sketch, right_hash):
    replicas = 1
    for axis in REP:
        replicas *= lax.axis_size(axis)
    rank = ((lax.axis_index("xh") + 1) % 2) * 4 + (lax.axis_index("y") + 2) % 4
    rank = rank.astype(jnp.int32).reshape(1)
    hashes = right_hash.reshape(1, -1)
    recv = exchange(sketch(rank, hashes, deltas, residual, left_sketch))
    recv = recv.reshape(8, ROW_SETS, (1 + LEFT_TILES) * KEPT, 128)
    reduced, left = reduce_columns(recv, left_sketch.shape[1])
    parts = sum_over_rings(reduced)
    back = expand_columns(parts, left, replicas).reshape(BLOCKS, KEPT, 128)
    projected = exchange(back).reshape(HALF, 128)
    return tuple(apply_update(hashes, projected, deltas, residual, momentum, params))


def solution(mesh):
    names, sizes = zip(*SIZES)
    fine = Mesh(mesh.devices.reshape(sizes), names)
    rows = P(None, FSDP, None)
    tall = P(REP, None, FSDP, None)
    return jax.shard_map(
        per_device,
        mesh=fine,
        in_specs=(tall, tall, rows, rows, P(FSDP, None), P()),
        out_specs=(rows, rows, tall),
        check_vma=False,
    )
```

time: 320 us -> 53.5 us (0.17)
  waiting for transfers between devices: 264 us -> 5.29 us
  matrix products: 39.6 us -> 0 us
  blocking collectives: 0 us -> 28.8 us
  between operations: 14.1 us -> 0.69 us
  starting transfers between devices: 0.04 us -> 10 us
  Pallas kernels: 0 us -> 8.51 us
    psum x1 -> x0, waiting for transfers between devices: 264 us -> none  [per_device(): total_sketch = lax.psum(partial_sketch, ('rep', 'fsdp')) / replicas]
    dot_general x4 -> x0, matrix products: 39.6 us -> none  [the longest x1 20.1 us: per_device(): update = jnp.einsum('mpk,nk->pmn', projected, signed, precision=highest)]
    all_to_all x0 -> x2, blocking collectives: none -> 28.8 us  [exchange(): return lax.all_to_all(x, AXES, 0, 0, axis_index_groups=plane_groups())]
    ppermute x0 -> x3, starting transfers between devices: none -> 10 us  [sum_over_rings(): swap = lambda v, pairs: lax.ppermute(v, 'zh', list(enumerate(pairs)))]
    pallas_call x0 -> x4, Pallas kernels: none -> 8.51 us  [the longest x1 5.1 us: apply_update(): pl.pallas_call(apply_kernel, in_specs=[VMEM_BLOCK] * 2 + [HBM_BLOCK] * 4,...]
    ppermute x0 -> x3, waiting for transfers between devices: none -> 5.29 us  [sum_over_rings(): swap = lambda v, pairs: lax.ppermute(v, 'zh', list(enumerate(pairs)))]
  transfers between devices with their start and end apart: 1 -> 3, of which waited for: 1 -> 3; matrix products, arithmetic and copies ran while one was open for 0% -> 0% of each run, Pallas kernels for 0% -> 0%
where the time goes in v2:
time: 53.5 us; the launch traced here: 53.4 us
  blocking collectives  28.8 us (54%)
  starting transfers between devices  10 us (19%)
  Pallas kernels  8.51 us (16%)
  waiting for transfers between devices  5.29 us (10%)
  between operations  0.69 us (1%)
    all_to_all x2, blocking collectives, exchange(): return lax.all_to_all(x, AXES, 0, 0, axis_index_groups=plane_groups())  28.8 us
    ppermute x3, starting transfers between devices, sum_over_rings(): swap = lambda v, pairs: lax.ppermute(v, 'zh', list(enumerate(pairs)))  10 us
    ppermute x3, waiting for transfers between devices, sum_over_rings(): swap = lambda v, pairs: lax.ppermute(v, 'zh', list(enumerate(pairs)))  5.29 us
    pallas_call x1, Pallas kernels, apply_update(): pl.pallas_call(apply_kernel, in_specs=[VMEM_BLOCK] * 2 + [HBM_BLOCK] * 4,...  5.1 us
    pallas_call x1, Pallas kernels, sketch(): pl.pallas_call(sketch_kernel, in_specs=[SMEM_BLOCK] + [HBM_BLOCK] * 4, ou...  2.91 us
  transfers between devices with their start and end apart: 3, of which 3 were waited for; matrix products, arithmetic and copies ran while one was open for 0% of the time, Pallas kernels for 0%

profile of v2, /device:TPU:1, one launch (start us, length us, event | category | flops | bytes accessed | tf_op | source)
XLA Modules:
  0.0 53.4 jit_solution(12940505128564418526)
XLA Ops:
  0.7 0.0 copy-start
  0.7 2.9 %sketch.1 = f32[32,24,128]{2,1,0:T(8,128)S(1)} custom-call(s32[1]{0:T(128)} %bitcast.1.rank_ref, s32[1,8192]{1,0:T(1,128)} %bitcast.8, bf16[1,2,32,8192]{3,2,1,0:T(8,128)(2,1)} %deltas_in.3, bf16[1,2,32,8192]{3,2,1,0:T(8,128)(2,1)} %residual_in.3, bf16[32,512]{1,0:T(8,128)(2,1)} %left_in.1), custom_call_target="tpu_custom_call" | custom-call | tf_op jit(solution)/shard_map/sketch/pallas_call | solution.py:108
  3.6 15.3 %all_to_all.10 = f32[32,24,128]{2,1,0:T(8,128)S(1)} all-to-all(f32[32,24,128]{2,1,0:T(8,128)S(1)} %sketch.1), channel_id=1, replica_groups={{193,192,195,194,225,224,227,226,129,128,131,130,161,160,163,162,65,64,..., dimensions={0} | all-to-all | bytes 786432 | tf_op jit(solution)/shard_map/all_to_all | solution.py:301
  18.9 0.2 reduce_columns.1
  19.1 1.6 %collective-permute-start = (f32[32,512]{1,0:T(8,128)S(1)}, f32[32,512]{1,0:T(8,128)S(1)}, u32[]{:S(2)}, u32[]{:S(2)}) collective-permute-start(f32[32,512]{1,0:T(8,128)S(1)} %get-tuple-element.5), channel_id=1, source_target_pairs={{0,4},{4,0},{8,12},{12,8},{16,20},{20,16},{24,28},{28,24},{1,5},{5... | collective-permute-start | bytes 196616 | tf_op jit(solution)/shard_map/ppermute | solution.py:279
  20.7 1.7 %collective-permute-done = f32[32,512]{1,0:T(8,128)S(1)} collective-permute-done((f32[32,512]{1,0:T(8,128)S(1)}, f32[32,512]{1,0:T(8,128)S(1)}, u32[]{:S(2)}, u32[]{:S(2)}) %collective-permute-start) | collective-permute-done | bytes 65568 | tf_op jit(solution)/shard_map/ppermute | solution.py:279
  22.3 3.1 %collective-permute-start.1 = (f32[32,512]{1,0:T(8,128)S(1)}, f32[32,512]{1,0:T(8,128)S(1)}, u32[]{:S(2)}, u32[]{:S(2)}) collective-permute-start(f32[32,512]{1,0:T(8,128)S(1)} %add.27), channel_id=1, source_target_pairs={{0,8},{4,12},{8,0},{12,4},{16,24},{20,28},{24,16},{28,20},{1,9},{5... | collective-permute-start | bytes 196616 | tf_op jit(solution)/shard_map/ppermute | solution.py:279
  25.4 1.7 %collective-permute-done.1 = f32[32,512]{1,0:T(8,128)S(1)} collective-permute-done((f32[32,512]{1,0:T(8,128)S(1)}, f32[32,512]{1,0:T(8,128)S(1)}, u32[]{:S(2)}, u32[]{:S(2)}) %collective-permute-start.1) | collective-permute-done | bytes 65568 | tf_op jit(solution)/shard_map/ppermute | solution.py:279
  27.1 5.4 %collective-permute-start.2 = (f32[32,512]{1,0:T(8,128)S(1)}, f32[32,512]{1,0:T(8,128)S(1)}, u32[]{:S(2)}, u32[]{:S(2)}) collective-permute-start(f32[32,512]{1,0:T(8,128)S(1)} %add.28.refs_0_), channel_id=1, source_target_pairs={{0,24},{4,28},{8,16},{12,20},{16,8},{20,12},{24,0},{28,4},{1,25},{... | collective-permute-start | bytes 196616 | tf_op jit(solution)/shard_map/ppermute | solution.py:279
  32.5 2.0 %collective-permute-done.2.refs_1_ = f32[32,512]{1,0:T(8,128)S(1)} collective-permute-done((f32[32,512]{1,0:T(8,128)S(1)}, f32[32,512]{1,0:T(8,128)S(1)}, u32[]{:S(2)}, u32[]{:S(2)}) %collective-permute-start.2) | collective-permute-done | bytes 65568 | tf_op jit(solution)/shard_map/ppermute | solution.py:279
  34.5 0.3 expand_columns.1
  34.8 13.5 %all_to_all.11 = f32[32,8,128]{2,1,0:T(8,128)S(1)} all-to-all(f32[32,8,128]{2,1,0:T(8,128)S(1)} %bitcast.7), channel_id=1, replica_groups={{193,192,195,194,225,224,227,226,129,128,131,130,161,160,163,162,65,64,..., dimensions={0} | all-to-all | bytes 262144 | tf_op jit(solution)/shard_map/all_to_all | solution.py:301
  48.3 0.0 copy-done
  48.3 5.1 %apply_update.1 = (f32[2,32,8192]{2,1,0:T(8,128)}, f32[2,32,8192]{2,1,0:T(8,128)}, bf16[1,2,32,8192]{3,2,1,0:T(8,128)(2,1)}) custom-call(s32[1,8192]{1,0:T(1,128)S(1)} %bitcast.9, f32[256,128]{1,0:T(8,128)S(1)} %bitcast.6, bf16[1,2,32,8192]{3,2,1,0:T(8,128)(2,1)} %deltas_in.3, bf16[1,2,32,8192]{3,2,1,0:T(8,128)(2,1)} %residual_in.3, ...), custom_call_target="tpu_custom_call" | custom-call | tf_op jit(solution)/shard_map/apply_update/pallas_call | solution.py:256
  (2 shorter events, 0.0 us)
Async XLA Ops:
  0.7 47.6 %copy-start = (s32[8192]{0:T(1024)S(1)}, s32[8192]{0:T(1024)}, u32[]{:S(2)}) copy-start(s32[8192]{0:T(1024)} %param.11) | copy-start | bytes 98308
  19.1 3.2 %collective-permute-start = (f32[32,512]{1,0:T(8,128)S(1)}, f32[32,512]{1,0:T(8,128)S(1)}, u32[]{:S(2)}, u32[]{:S(2)}) collective-permute-start(f32[32,512]{1,0:T(8,128)S(1)} %get-tuple-element.5), channel_id=1, source_target_pairs={{0,4},{4,0},{8,12},{12,8},{16,20},{20,16},{24,28},{28,24},{1,5},{5... | collective-permute-start | bytes 196616 | tf_op jit(solution)/shard_map/ppermute | solution.py:279
  22.3 4.7 %collective-permute-start.1 = (f32[32,512]{1,0:T(8,128)S(1)}, f32[32,512]{1,0:T(8,128)S(1)}, u32[]{:S(2)}, u32[]{:S(2)}) collective-permute-start(f32[32,512]{1,0:T(8,128)S(1)} %add.27), channel_id=1, source_target_pairs={{0,8},{4,12},{8,0},{12,4},{16,24},{20,28},{24,16},{28,20},{1,9},{5... | collective-permute-start | bytes 196616 | tf_op jit(solution)/shard_map/ppermute | solution.py:279
  27.1 7.4 %collective-permute-start.2 = (f32[32,512]{1,0:T(8,128)S(1)}, f32[32,512]{1,0:T(8,128)S(1)}, u32[]{:S(2)}, u32[]{:S(2)}) collective-permute-start(f32[32,512]{1,0:T(8,128)S(1)} %add.28.refs_0_), channel_id=1, source_target_pairs={{0,24},{4,28},{8,16},{12,20},{16,8},{20,12},{24,0},{28,4},{1,25},{... | collective-permute-start | bytes 196616 | tf_op jit(solution)/shard_map/ppermute | solution.py:279

commit v3 on v2

--- a/solution.py
+++ b/solution.py
@@ -24,6 +24,7 @@
 KEPT = HALF // BLOCKS
 LEFT_TILES = 2
 CHUNK = 2048
+FETCHED = 4096
 NT = (((1,), (1,)), ((), ()))
 VMEM_BLOCK = pl.BlockSpec(memory_space=pltpu.VMEM)
 HBM_BLOCK = pl.BlockSpec(memory_space=pltpu.HBM)
@@ -164,7 +165,7 @@
 
 
 def expand_kernel(terms, replicas, *refs):
-    parts, left_ref, out_ref = refs[:terms], refs[terms], refs[terms + 1]
+    parts, left_ref, out_ref = refs[:terms], refs[terms], refs[-1]
     mask = quarter_mask(4 * KEPT)
     c = parts[0][...]
     for part in parts[1:]:
@@ -183,106 +184,132 @@
         out_ref[rep * rows.shape[0] : (rep + 1) * rows.shape[0]] = rows
 
 
-def expand_columns(parts, left, replicas):
+def expand_columns(parts, left, token, replicas):
     return pl.pallas_call(
         functools.partial(expand_kernel, len(parts), replicas),
-        in_specs=[VMEM_BLOCK] * (len(parts) + 1),
+        in_specs=[VMEM_BLOCK] * (len(parts) + 2),
         out_specs=VMEM_BLOCK,
         out_shape=pltpu.VMEM((HALF, 128), jnp.float32),
         compiler_params=SMALL,
         name="expand_columns",
-    )(*[in_vmem(x) for x in (*parts, left)])
+    )(*[in_vmem(x) for x in (*parts, left, token)])
+
+
+def columns(ref, at):
+    return ref.at[(slice(None),) * (len(ref.shape) - 1) + (at,)]
+
+
+def fetch_kernel(after_ref, *refs):
+    count = (len(refs) - 2) // 2
+    done_ref, sems = refs[count], refs[-1]
+    copies = []
+    for i, (there, here) in enumerate(zip(refs[:count], refs[count + 1 : -1])):
+        there = columns(there, pl.ds(0, here.shape[-1]))
+        copies.append(pltpu.make_async_copy(there, here, sems.at[i]))
+        copies[-1].start()
+    done_ref[...] = after_ref[:8, :128]
+    for copy in copies:
+        copy.wait()
+
+
+def fetch(after, arrays):
+    return pl.pallas_call(
+        fetch_kernel,
+        in_specs=[VMEM_BLOCK] + [HBM_BLOCK] * len(arrays),
+        out_specs=[VMEM_BLOCK] * (len(arrays) + 1),
+        out_shape=[
+            pltpu.VMEM((8, 128), jnp.float32),
+            *[pltpu.VMEM(x.shape[:-1] + (FETCHED,), x.dtype) for x in arrays],
+        ],
+        scratch_shapes=[pltpu.SemaphoreType.DMA((len(arrays),))],
+        compiler_params=SMALL,
+        cost_estimate=pl.CostEstimate(
+            flops=0, bytes_accessed=6 * 2**20, transcendentals=0
+        ),
+        name="fetch",
+    )(in_vmem(after), *map(in_hbm, arrays))
 
 
 def apply_kernel(
-    hash_ref, p_ref, deltas_in, residual_in, momentum_in, params_in,
-    params_out, momentum_out, residual_out,
-    deltas_ref, residual_ref, momentum_ref, params_ref,
-    new_params_ref, new_momentum_ref, new_residual_ref, in_sems, out_sems,
+    hash_ref, p_ref, *refs
 ):
+    early, inputs, outputs, late, results = (refs[i : i + 4] for i in (0, 4, 8, 11, 15))
+    outputs, results = outputs[:3], results[:3]
+    in_sems, out_sems = refs[18:]
     count = hash_ref.shape[1] // CHUNK
-
-    def cut(ref, j):
-        return ref.at[(slice(None),) * (len(ref.shape) - 1) + (pl.ds(j * CHUNK, CHUNK),)]
-
-    pairs = (
-        (deltas_in, deltas_ref), (residual_in, residual_ref),
-        (momentum_in, momentum_ref), (params_in, params_ref),
-    )
-    loads = [
-        [
-            pltpu.make_async_copy(cut(there, j), cut(here, j), in_sems.at[i, j])
-            for i, (there, here) in enumerate(pairs)
-        ]
-        for j in range(count)
-    ]
-    for group in loads:
-        for copy in group:
-            copy.start()
+    ready = FETCHED // CHUNK
+    loads = []
+    for j in range(ready, count):
+        group = []
+        for i, (there, here) in enumerate(zip(inputs, late)):
+            there = columns(there, pl.ds(j * CHUNK, CHUNK))
+            here = columns(here, pl.ds(j * CHUNK - FETCHED, CHUNK))
+            group.append(pltpu.make_async_copy(there, here, in_sems.at[i, j - ready]))
+            group[-1].start()
+        loads.append(group)
     left = split(p_ref[...].T)
     rows = left.shape[0] // 4
     stores = []
-    for j in range(count):
+    order = [j + k for j in range(ready) for k in (0, ready)]
+    for j in order:
         at = pl.ds(j * CHUNK, CHUNK)
         low, upper, sign = hash_parts(hash_ref[:, at])
         both = jnp.dot(left, onehot(low, CHUNK), preferred_element_type=jnp.float32)
         both = both[: 2 * rows] + both[2 * rows :]
         u = jnp.where(upper, both[rows:], both[:rows]) * sign
-        u = u.reshape(params_ref.shape[:2] + (CHUNK,))
-        for copy in loads[j]:
-            copy.wait()
-        d = deltas_ref[0, :, :, at].astype(jnp.float32)
-        acc = residual_ref[0, :, :, at].astype(jnp.float32) + d
-        new_residual_ref[0, :, :, at] = (acc - u).astype(jnp.bfloat16)
-        new_momentum = 0.9 * momentum_ref[:, :, at] + u
-        new_momentum_ref[:, :, at] = new_momentum
-        new_params_ref[:, :, at] = params_ref[:, :, at] - 0.7 * (u + 0.9 * new_momentum)
-        pairs = (
-            (new_residual_ref, residual_out),
-            (new_momentum_ref, momentum_out),
-            (new_params_ref, params_out),
-        )
-        for i, (here, there) in enumerate(pairs):
-            copy = pltpu.make_async_copy(cut(here, j), cut(there, j), out_sems.at[i, j])
+        u = u.reshape(early[3].shape[:2] + (CHUNK,))
+        if j >= ready:
+            for copy in loads[j - ready]:
+                copy.wait()
+        source = early if j < ready else late
+        there = pl.ds(j * CHUNK - (0 if j < ready else FETCHED), CHUNK)
+        d, r, m, p = (ref[(slice(None),) * (len(ref.shape) - 1) + (there,)] for ref in source)
+        acc = r[0].astype(jnp.float32) + d[0].astype(jnp.float32)
+        new_residual = (acc - u).astype(jnp.bfloat16)
+        new_momentum = 0.9 * m + u
+        new_params = p - 0.7 * (u + 0.9 * new_momentum)
+        results[2][0, :, :, at] = new_residual
+        results[1][:, :, at] = new_momentum
+        results[0][:, :, at] = new_params
+        for i in (2, 1, 0):
+            copy = pltpu.make_async_copy(
+                columns(results[i], at), columns(outputs[i], at), out_sems.at[i, j]
+            )
             copy.start()
             stores.append(copy)
     for copy in stores:
         copy.wait()
 
 
-def apply_update(hashes, projected, deltas, residual, momentum, params):
-    wide, narrow = pltpu.VMEM(params.shape, params.dtype), pltpu.VMEM(deltas.shape, deltas.dtype)
+def apply_update(hashes, projected, early, arrays):
+    deltas, _, momentum, params = arrays
     count = params.shape[2] // CHUNK
+    ready = FETCHED // CHUNK
+    late = [
+        pltpu.VMEM(x.shape[:-1] + (x.shape[-1] - FETCHED,), x.dtype) for x in arrays
+    ]
+    results = [params, momentum, deltas]
     return pl.pallas_call(
         apply_kernel,
-        in_specs=[VMEM_BLOCK] * 2 + [HBM_BLOCK] * 4,
+        in_specs=[VMEM_BLOCK] * 6 + [HBM_BLOCK] * 4,
         out_specs=[HBM_BLOCK] * 3,
-        out_shape=[
-            jax.ShapeDtypeStruct(params.shape, jnp.float32),
-            jax.ShapeDtypeStruct(momentum.shape, jnp.float32),
-            jax.ShapeDtypeStruct(residual.shape, jnp.bfloat16),
-        ],
+        out_shape=[jax.ShapeDtypeStruct(x.shape, x.dtype) for x in results],
         scratch_shapes=[
-            narrow, narrow, wide, wide, wide, wide, narrow,
-            pltpu.SemaphoreType.DMA((4, count)),
+            *late,
+            *[pltpu.VMEM(x.shape, x.dtype) for x in results],
+            pltpu.SemaphoreType.DMA((4, count - ready)),
             pltpu.SemaphoreType.DMA((3, count)),
         ],
         compiler_params=PARAMS,
         name="apply_update",
-    )(
-        in_vmem(hashes), in_vmem(projected),
-        *[in_hbm(x) for x in (deltas, residual, momentum, params)],
-    )
+    )(in_vmem(hashes), in_vmem(projected), *map(in_vmem, early), *map(in_hbm, arrays))
 
 
 def sum_over_rings(x):
     swap = lambda v, pairs: lax.ppermute(v, "zh", list(enumerate(pairs)))
-    if RINGS == 8:
-        x = x + swap(x, [1, 0, 3, 2, 5, 4, 7, 6])
-        x = x + swap(x, [2, 3, 0, 1, 6, 7, 4, 5])
-        return x, swap(x, [6, 7, 4, 5, 2, 3, 0, 1])
-    x = x + swap(x, [1, 0, 3, 2])
-    return x, swap(x, [3, 2, 1, 0])
+    far = swap(x, [3, 2, 1, 0, 7, 6, 5, 4])
+    x = x + swap(x, [1, 0, 3, 2, 5, 4, 7, 6]) + swap(x, [2, 3, 0, 1, 6, 7, 4, 5]) + far
+    return x, (x, swap(x, [6, 7, 4, 5, 2, 3, 0, 1]))
 
 
 AXES = tuple(name for name, _ in SIZES)
@@ -311,10 +338,12 @@
     recv = exchange(sketch(rank, hashes, deltas, residual, left_sketch))
     recv = recv.reshape(8, ROW_SETS, (1 + LEFT_TILES) * KEPT, 128)
     reduced, left = reduce_columns(recv, left_sketch.shape[1])
-    parts = sum_over_rings(reduced)
-    back = expand_columns(parts, left, replicas).reshape(BLOCKS, KEPT, 128)
+    arrays = (deltas, residual, momentum, params)
+    middle, parts = sum_over_rings(reduced)
+    token, *early = fetch(middle, arrays)
+    back = expand_columns(parts, left, token, replicas).reshape(BLOCKS, KEPT, 128)
     projected = exchange(back).reshape(HALF, 128)
-    return tuple(apply_update(hashes, projected, deltas, residual, momentum, params))
+    return tuple(apply_update(hashes, projected, early, arrays))
 
 
 def solution(mesh):

time: 53.5 us -> 50.8 us (0.950)
  starting transfers between devices: 10 us -> 8.42 us
  blocking collectives: 28.8 us -> 27.7 us
  waiting for transfers between devices: 5.29 us -> 4.51 us
  Pallas kernels: 8.51 us -> 9.2 us
    ppermute x3 -> x4, starting transfers between devices: 10 us -> 8.42 us  [sum_over_rings(): swap = lambda v, pairs: lax.ppermute(v, 'zh', list(enumerate(pairs)))]
    all_to_all x2, blocking collectives: 28.8 us -> 27.7 us  [exchange(): return lax.all_to_all(x, AXES, 0, 0, axis_index_groups=plane_groups())]
    ppermute x3 -> x4, waiting for transfers between devices: 5.29 us -> 4.51 us  [sum_over_rings(): swap = lambda v, pairs: lax.ppermute(v, 'zh', list(enumerate(pairs)))]
    pallas_call x1 -> x2, Pallas kernels: 5.1 us -> 5.79 us  [the longest x1 3.89 us: apply_update(): pl.pallas_call(apply_kernel, in_specs=[VMEM_BLOCK] * 6 + [HBM_BLOCK] * 4,...]
  transfers between devices with their start and end apart: 3 -> 4, of which waited for: 3 -> 2; matrix products, arithmetic and copies ran while one was open for 0% -> 0% of each run, Pallas kernels for 0% -> 4%
where the time goes in v3:
time: 50.8 us; the launch traced here: 50.6 us
  blocking collectives  27.7 us (55%)
  Pallas kernels  9.2 us (18%)
  starting transfers between devices  8.42 us (17%)
  waiting for transfers between devices  4.51 us (9%)
  between operations  0.7 us (1%)
    all_to_all x2, blocking collectives, exchange(): return lax.all_to_all(x, AXES, 0, 0, axis_index_groups=plane_groups())  27.7 us
    ppermute x4, starting transfers between devices, sum_over_rings(): swap = lambda v, pairs: lax.ppermute(v, 'zh', list(enumerate(pairs)))  8.42 us
    ppermute x4, waiting for transfers between devices, sum_over_rings(): swap = lambda v, pairs: lax.ppermute(v, 'zh', list(enumerate(pairs)))  4.51 us
    pallas_call x1, Pallas kernels, apply_update(): pl.pallas_call(apply_kernel, in_specs=[VMEM_BLOCK] * 6 + [HBM_BLOCK] * 4,...  3.89 us
    pallas_call x1, Pallas kernels, sketch(): pl.pallas_call(sketch_kernel, in_specs=[SMEM_BLOCK] + [HBM_BLOCK] * 4, ou...  2.91 us
    pallas_call x1, Pallas kernels, fetch(): pl.pallas_call(fetch_kernel, in_specs=[VMEM_BLOCK] + [HBM_BLOCK] * len(ar...  1.9 us
  transfers between devices with their start and end apart: 4, of which 2 were waited for; matrix products, arithmetic and copies ran while one was open for 0% of the time, Pallas kernels for 4%

profile of v3, /device:TPU:1, one launch (start us, length us, event | category | flops | bytes accessed | tf_op | source)
XLA Modules:
  0.0 50.6 jit_solution(12265515416693108434)
XLA Ops:
  0.7 2.9 %sketch.1 = f32[32,24,128]{2,1,0:T(8,128)S(1)} custom-call(s32[1]{0:T(128)} %bitcast.1.rank_ref, s32[1,8192]{1,0:T(1,128)} %bitcast.8, bf16[1,2,32,8192]{3,2,1,0:T(8,128)(2,1)} %refs_4_.1, bf16[1,2,32,8192]{3,2,1,0:T(8,128)(2,1)} %refs_5_.1, bf16[32,512]{1,0:T(8,128)(2,1)} %left_in.1), custom_call_target="tpu_custom_call" | custom-call | tf_op jit(solution)/shard_map/sketch/pallas_call | solution.py:109
  3.6 15.3 %all_to_all.10 = f32[32,24,128]{2,1,0:T(8,128)S(1)} all-to-all(f32[32,24,128]{2,1,0:T(8,128)S(1)} %sketch.1), channel_id=1, replica_groups={{193,192,195,194,225,224,227,226,129,128,131,130,161,160,163,162,65,64,..., dimensions={0} | all-to-all | bytes 786432 | tf_op jit(solution)/shard_map/all_to_all | solution.py:328
  18.9 0.2 reduce_columns.1
  19.1 4.3 %collective-permute-start.2 = (f32[32,512]{1,0:T(8,128)S(1)}, f32[32,512]{1,0:T(8,128)S(1)}, u32[]{:S(2)}, u32[]{:S(2)}) collective-permute-start(f32[32,512]{1,0:T(8,128)S(1)} %get-tuple-element.10), channel_id=1, source_target_pairs={{0,12},{4,8},{8,4},{12,0},{16,28},{20,24},{24,20},{28,16},{1,13},{... | collective-permute-start | bytes 196616 | tf_op jit(solution)/shard_map/ppermute | solution.py:309
  23.3 0.0 collective-permute-start.1
  23.4 0.4 collective-permute-start
  23.7 1.4 %collective-permute-done.2 = f32[32,512]{1,0:T(8,128)S(1)} collective-permute-done((f32[32,512]{1,0:T(8,128)S(1)}, f32[32,512]{1,0:T(8,128)S(1)}, u32[]{:S(2)}, u32[]{:S(2)}) %collective-permute-start.2) | collective-permute-done | bytes 65568 | tf_op jit(solution)/shard_map/ppermute | solution.py:309
  25.1 3.1 %collective-permute-done.1 = f32[32,512]{1,0:T(8,128)S(1)} collective-permute-done((f32[32,512]{1,0:T(8,128)S(1)}, f32[32,512]{1,0:T(8,128)S(1)}, u32[]{:S(2)}, u32[]{:S(2)}) %collective-permute-start.1) | collective-permute-done | bytes 65568 | tf_op jit(solution)/shard_map/ppermute | solution.py:309
  28.2 0.0 collective-permute-done
  28.2 0.0 copy-start
  28.3 3.8 %collective-permute-start.3 = (f32[32,512]{1,0:T(8,128)S(1)}, f32[32,512]{1,0:T(8,128)S(1)}, u32[]{:S(2)}, u32[]{:S(2)}) collective-permute-start(f32[32,512]{1,0:T(8,128)S(1)} %add_add_fusion.after_ref.refs_0_), channel_id=1, source_target_pairs={{0,24},{4,28},{8,16},{12,20},{16,8},{20,12},{24,0},{28,4},{1,25},{... | collective-permute-start | bytes 196616 | tf_op jit(solution)/shard_map/ppermute | solution.py:309
  32.0 1.9 %fetch.1 = (f32[8,128]{1,0:T(8,128)S(1)}, bf16[1,2,32,4096]{3,2,1,0:T(8,128)(2,1)S(1)}, bf16[1,2,32,4096]{3,2,1,0:T(8,128)(2,1)S(1)}, f32[2,32,4096]{2,1,0:T(8,128)S(1)}, f32[2,32,4096]{2,1,0:T(8,128)S(1)}) custom-call(f32[32,512]{1,0:T(8,128)S(1)} %add_add_fusion.after_ref.refs_0_, bf16[1,2,32,8192]{3,2,1,0:T(8,128)(2,1)} %refs_4_.1, ...), custom_call_target="tpu_custom_call" | custom-call | bytes 6291456 | tf_op jit(solution)/shard_map/fetch/pallas_call | solution.py:216
  34.0 0.0 collective-permute-done.3.refs_1_
  34.0 0.3 expand_columns.1
  34.3 12.4 %all_to_all.11 = f32[32,8,128]{2,1,0:T(8,128)S(1)} all-to-all(f32[32,8,128]{2,1,0:T(8,128)S(1)} %bitcast.7), channel_id=1, replica_groups={{193,192,195,194,225,224,227,226,129,128,131,130,161,160,163,162,65,64,..., dimensions={0} | all-to-all | bytes 262144 | tf_op jit(solution)/shard_map/all_to_all | solution.py:328
  46.7 0.0 copy-done
  46.7 3.9 %apply_update.1 = (f32[2,32,8192]{2,1,0:T(8,128)}, f32[2,32,8192]{2,1,0:T(8,128)}, bf16[1,2,32,8192]{3,2,1,0:T(8,128)(2,1)}) custom-call(s32[1,8192]{1,0:T(1,128)S(1)} %bitcast.9, f32[256,128]{1,0:T(8,128)S(1)} %bitcast.6, bf16[1,2,32,4096]{3,2,1,0:T(8,128)(2,1)S(1)} %get-tuple-element.13.refs_0_, bf16[1,2,32,4096]{3,2,1,0:T(8,128)(2,1)S(1)} %get-tuple-element.14.refs_1_, ...), custom_call_target="tpu_custom_call" | custom-call | tf_op jit(solution)/shard_map/apply_update/pallas_call | solution.py:292
  (1 shorter events, 0.0 us)
Async XLA Ops:
  19.1 6.0 %collective-permute-start.2 = (f32[32,512]{1,0:T(8,128)S(1)}, f32[32,512]{1,0:T(8,128)S(1)}, u32[]{:S(2)}, u32[]{:S(2)}) collective-permute-start(f32[32,512]{1,0:T(8,128)S(1)} %get-tuple-element.10), channel_id=1, source_target_pairs={{0,12},{4,8},{8,4},{12,0},{16,28},{20,24},{24,20},{28,16},{1,13},{... | collective-permute-start | bytes 196616 | tf_op jit(solution)/shard_map/ppermute | solution.py:309
  23.3 4.9 %collective-permute-start.1 = (f32[32,512]{1,0:T(8,128)S(1)}, f32[32,512]{1,0:T(8,128)S(1)}, u32[]{:S(2)}, u32[]{:S(2)}) collective-permute-start(f32[32,512]{1,0:T(8,128)S(1)} %get-tuple-element.10), channel_id=1, source_target_pairs={{0,8},{4,12},{8,0},{12,4},{16,24},{20,28},{24,16},{28,20},{1,9},{5... | collective-permute-start | bytes 196616 | tf_op jit(solution)/shard_map/ppermute | solution.py:309
  23.4 4.9 %collective-permute-start = (f32[32,512]{1,0:T(8,128)S(1)}, f32[32,512]{1,0:T(8,128)S(1)}, u32[]{:S(2)}, u32[]{:S(2)}) collective-permute-start(f32[32,512]{1,0:T(8,128)S(1)} %get-tuple-element.10), channel_id=1, source_target_pairs={{0,4},{4,0},{8,12},{12,8},{16,20},{20,16},{24,28},{28,24},{1,5},{5... | collective-permute-start | bytes 196616 | tf_op jit(solution)/shard_map/ppermute | solution.py:309
  28.2 18.5 %copy-start = (s32[8192]{0:T(1024)S(1)}, s32[8192]{0:T(1024)}, u32[]{:S(2)}) copy-start(s32[8192]{0:T(1024)} %param.11) | copy-start | bytes 98308
  28.3 5.7 %collective-permute-start.3 = (f32[32,512]{1,0:T(8,128)S(1)}, f32[32,512]{1,0:T(8,128)S(1)}, u32[]{:S(2)}, u32[]{:S(2)}) collective-permute-start(f32[32,512]{1,0:T(8,128)S(1)} %add_add_fusion.after_ref.refs_0_), channel_id=1, source_target_pairs={{0,24},{4,28},{8,16},{12,20},{16,8},{20,12},{24,0},{28,4},{1,25},{... | collective-permute-start | bytes 196616 | tf_op jit(solution)/shard_map/ppermute | solution.py:309

commit v4 on v3

--- a/solution.py
+++ b/solution.py
@@ -134,7 +134,7 @@
         rows = []
         for i in range(0, 8, 2):
             tiles = [
-                recv_ref[i + j, f, (t + 1) * KEPT : (t + 2) * KEPT, :]
+                recv_ref[f, i + j, (t + 1) * KEPT : (t + 2) * KEPT, :]
                 for j in range(2)
                 for t in range(LEFT_TILES)
             ]
@@ -143,7 +143,7 @@
         for q in range(4):
             at = (4 * f + q) * rows.shape[0]
             left_ref[at : at + rows.shape[0]] = rows
-        part = jnp.sum(recv_ref[:, f, :KEPT, :], axis=0)
+        part = jnp.sum(recv_ref[f, :, :KEPT, :], axis=0)
         wide.append(jnp.where(mask, jnp.concatenate([part] * 4, axis=0), 0.0))
     wide = split(jnp.concatenate(wide, axis=1))
     t = jnp.dot(wide, left_ref[...], preferred_element_type=jnp.float32)
@@ -174,14 +174,13 @@
         split(c / replicas), left_ref[...], NT, preferred_element_type=jnp.float32
     )
     wide = wide[: 4 * KEPT] + wide[4 * KEPT :]
-    rows = []
     for f in range(ROW_SETS):
         t = jnp.where(mask, wide[:, f * 128 : (f + 1) * 128], 0.0)
         t = t[: 2 * KEPT] + t[2 * KEPT :]
-        rows.append(t[:KEPT] + t[KEPT:])
-    rows = jnp.concatenate(rows, axis=0)
-    for rep in range(8):
-        out_ref[rep * rows.shape[0] : (rep + 1) * rows.shape[0]] = rows
+        rows = t[:KEPT] + t[KEPT:]
+        for rep in range(8):
+            at = (8 * f + rep) * KEPT
+            out_ref[at : at + KEPT] = rows
 
 
 def expand_columns(parts, left, token, replicas):
@@ -320,7 +319,7 @@
     ids = np.arange(256).reshape([size for _, size in SIZES])
     if FLIP:
         ids = np.roll(ids, (1, 2, 1), (0, 1, 5))
-    ids = np.moveaxis(ids, 2, 0).reshape(RINGS, -1)
+    ids = ids.transpose(2, 3, 4, 5, 0, 1).reshape(RINGS, -1)
     return ids.tolist()
 
 
@@ -336,7 +335,7 @@
     rank = rank.astype(jnp.int32).reshape(1)
     hashes = right_hash.reshape(1, -1)
     recv = exchange(sketch(rank, hashes, deltas, residual, left_sketch))
-    recv = recv.reshape(8, ROW_SETS, (1 + LEFT_TILES) * KEPT, 128)
+    recv = recv.reshape(ROW_SETS, 8, (1 + LEFT_TILES) * KEPT, 128)
     reduced, left = reduce_columns(recv, left_sketch.shape[1])
     arrays = (deltas, residual, momentum, params)
     middle, parts = sum_over_rings(reduced)

time: 50.8 us -> 50.7 us (level)
  transfers between devices with their start and end apart: 4 -> 4, of which waited for: 2 -> 3; matrix products, arithmetic and copies ran while one was open for 0% -> 0% of each run, Pallas kernels for 4% -> 4%
where the time goes in v4:
time: 50.7 us; the launch traced here: 50.5 us
  blocking collectives  27.6 us (54%)
  Pallas kernels  9.2 us (18%)
  starting transfers between devices  8.3 us (16%)
  waiting for transfers between devices  4.67 us (9%)
  between operations  0.69 us (1%)
    all_to_all x2, blocking collectives, exchange(): return lax.all_to_all(x, AXES, 0, 0, axis_index_groups=plane_groups())  27.6 us
    ppermute x4, starting transfers between devices, sum_over_rings(): swap = lambda v, pairs: lax.ppermute(v, 'zh', list(enumerate(pairs)))  8.3 us
    ppermute x4, waiting for transfers between devices, sum_over_rings(): swap = lambda v, pairs: lax.ppermute(v, 'zh', list(enumerate(pairs)))  4.67 us
    pallas_call x1, Pallas kernels, apply_update(): pl.pallas_call(apply_kernel, in_specs=[VMEM_BLOCK] * 6 + [HBM_BLOCK] * 4,...  3.89 us
    pallas_call x1, Pallas kernels, sketch(): pl.pallas_call(sketch_kernel, in_specs=[SMEM_BLOCK] + [HBM_BLOCK] * 4, ou...  2.91 us
    pallas_call x1, Pallas kernels, fetch(): pl.pallas_call(fetch_kernel, in_specs=[VMEM_BLOCK] + [HBM_BLOCK] * len(ar...  1.9 us
  transfers between devices with their start and end apart: 4, of which 3 were waited for; matrix products, arithmetic and copies ran while one was open for 0% of the time, Pallas kernels for 4%

profile of v4, /device:TPU:1, one launch (start us, length us, event | category | flops | bytes accessed | tf_op | source)
XLA Modules:
  0.0 50.5 jit_solution(410219700386455478)
XLA Ops:
  0.7 2.9 %sketch.1 = f32[32,24,128]{2,1,0:T(8,128)S(1)} custom-call(s32[1]{0:T(128)} %bitcast.1.rank_ref, s32[1,8192]{1,0:T(1,128)} %bitcast.8, bf16[1,2,32,8192]{3,2,1,0:T(8,128)(2,1)} %refs_4_.1, bf16[1,2,32,8192]{3,2,1,0:T(8,128)(2,1)} %refs_5_.1, bf16[32,512]{1,0:T(8,128)(2,1)} %left_in.1), custom_call_target="tpu_custom_call" | custom-call | tf_op jit(solution)/shard_map/sketch/pallas_call | solution.py:109
  3.6 15.3 %all_to_all.10 = f32[32,24,128]{2,1,0:T(8,128)S(1)} all-to-all(f32[32,24,128]{2,1,0:T(8,128)S(1)} %sketch.1), channel_id=1, replica_groups={{193,225,129,161,65,97,1,33,192,224,128,160,64,96,0,32,195,227,131,163,..., dimensions={0} | all-to-all | bytes 786432 | tf_op jit(solution)/shard_map/all_to_all | solution.py:327
  18.8 0.2 reduce_columns.1
  19.1 4.3 %collective-permute-start.2 = (f32[32,512]{1,0:T(8,128)S(1)}, f32[32,512]{1,0:T(8,128)S(1)}, u32[]{:S(2)}, u32[]{:S(2)}) collective-permute-start(f32[32,512]{1,0:T(8,128)S(1)} %get-tuple-element.10), channel_id=1, source_target_pairs={{0,12},{4,8},{8,4},{12,0},{16,28},{20,24},{24,20},{28,16},{1,13},{... | collective-permute-start | bytes 196616 | tf_op jit(solution)/shard_map/ppermute | solution.py:308
  23.3 0.0 collective-permute-start.1
  23.3 0.4 collective-permute-start
  23.7 1.4 %collective-permute-done.2 = f32[32,512]{1,0:T(8,128)S(1)} collective-permute-done((f32[32,512]{1,0:T(8,128)S(1)}, f32[32,512]{1,0:T(8,128)S(1)}, u32[]{:S(2)}, u32[]{:S(2)}) %collective-permute-start.2) | collective-permute-done | bytes 65568 | tf_op jit(solution)/shard_map/ppermute | solution.py:308
  25.1 3.2 %collective-permute-done.1 = f32[32,512]{1,0:T(8,128)S(1)} collective-permute-done((f32[32,512]{1,0:T(8,128)S(1)}, f32[32,512]{1,0:T(8,128)S(1)}, u32[]{:S(2)}, u32[]{:S(2)}) %collective-permute-start.1) | collective-permute-done | bytes 65568 | tf_op jit(solution)/shard_map/ppermute | solution.py:308
  28.3 0.0 collective-permute-done
  28.3 0.0 copy-start
  28.3 3.7 %collective-permute-start.3 = (f32[32,512]{1,0:T(8,128)S(1)}, f32[32,512]{1,0:T(8,128)S(1)}, u32[]{:S(2)}, u32[]{:S(2)}) collective-permute-start(f32[32,512]{1,0:T(8,128)S(1)} %add_add_fusion.after_ref.refs_0_), channel_id=1, source_target_pairs={{0,24},{4,28},{8,16},{12,20},{16,8},{20,12},{24,0},{28,4},{1,25},{... | collective-permute-start | bytes 196616 | tf_op jit(solution)/shard_map/ppermute | solution.py:308
  32.0 1.9 %fetch.1 = (f32[8,128]{1,0:T(8,128)S(1)}, bf16[1,2,32,4096]{3,2,1,0:T(8,128)(2,1)S(1)}, bf16[1,2,32,4096]{3,2,1,0:T(8,128)(2,1)S(1)}, f32[2,32,4096]{2,1,0:T(8,128)S(1)}, f32[2,32,4096]{2,1,0:T(8,128)S(1)}) custom-call(f32[32,512]{1,0:T(8,128)S(1)} %add_add_fusion.after_ref.refs_0_, bf16[1,2,32,8192]{3,2,1,0:T(8,128)(2,1)} %refs_4_.1, ...), custom_call_target="tpu_custom_call" | custom-call | bytes 6291456 | tf_op jit(solution)/shard_map/fetch/pallas_call | solution.py:215
  33.9 0.1 collective-permute-done.3.refs_1_
  34.0 0.3 expand_columns.1
  34.3 12.3 %all_to_all.11 = f32[32,8,128]{2,1,0:T(8,128)S(1)} all-to-all(f32[32,8,128]{2,1,0:T(8,128)S(1)} %bitcast.7), channel_id=1, replica_groups={{193,225,129,161,65,97,1,33,192,224,128,160,64,96,0,32,195,227,131,163,..., dimensions={0} | all-to-all | bytes 262144 | tf_op jit(solution)/shard_map/all_to_all | solution.py:327
  46.6 0.0 copy-done
  46.6 3.9 %apply_update.1 = (f32[2,32,8192]{2,1,0:T(8,128)}, f32[2,32,8192]{2,1,0:T(8,128)}, bf16[1,2,32,8192]{3,2,1,0:T(8,128)(2,1)}) custom-call(s32[1,8192]{1,0:T(1,128)S(1)} %bitcast.9, f32[256,128]{1,0:T(8,128)S(1)} %bitcast.6, bf16[1,2,32,4096]{3,2,1,0:T(8,128)(2,1)S(1)} %get-tuple-element.13.refs_0_, bf16[1,2,32,4096]{3,2,1,0:T(8,128)(2,1)S(1)} %get-tuple-element.14.refs_1_, ...), custom_call_target="tpu_custom_call" | custom-call | tf_op jit(solution)/shard_map/apply_update/pallas_call | solution.py:291
  (1 shorter events, 0.0 us)
Async XLA Ops:
  19.1 6.0 %collective-permute-start.2 = (f32[32,512]{1,0:T(8,128)S(1)}, f32[32,512]{1,0:T(8,128)S(1)}, u32[]{:S(2)}, u32[]{:S(2)}) collective-permute-start(f32[32,512]{1,0:T(8,128)S(1)} %get-tuple-element.10), channel_id=1, source_target_pairs={{0,12},{4,8},{8,4},{12,0},{16,28},{20,24},{24,20},{28,16},{1,13},{... | collective-permute-start | bytes 196616 | tf_op jit(solution)/shard_map/ppermute | solution.py:308
  23.3 5.0 %collective-permute-start.1 = (f32[32,512]{1,0:T(8,128)S(1)}, f32[32,512]{1,0:T(8,128)S(1)}, u32[]{:S(2)}, u32[]{:S(2)}) collective-permute-start(f32[32,512]{1,0:T(8,128)S(1)} %get-tuple-element.10), channel_id=1, source_target_pairs={{0,8},{4,12},{8,0},{12,4},{16,24},{20,28},{24,16},{28,20},{1,9},{5... | collective-permute-start | bytes 196616 | tf_op jit(solution)/shard_map/ppermute | solution.py:308
  23.3 5.0 %collective-permute-start = (f32[32,512]{1,0:T(8,128)S(1)}, f32[32,512]{1,0:T(8,128)S(1)}, u32[]{:S(2)}, u32[]{:S(2)}) collective-permute-start(f32[32,512]{1,0:T(8,128)S(1)} %get-tuple-element.10), channel_id=1, source_target_pairs={{0,4},{4,0},{8,12},{12,8},{16,20},{20,16},{24,28},{28,24},{1,5},{5... | collective-permute-start | bytes 196616 | tf_op jit(solution)/shard_map/ppermute | solution.py:308
  28.3 18.3 %copy-start = (s32[8192]{0:T(1024)S(1)}, s32[8192]{0:T(1024)}, u32[]{:S(2)}) copy-start(s32[8192]{0:T(1024)} %param.11) | copy-start | bytes 98308
  28.3 5.6 %collective-permute-start.3 = (f32[32,512]{1,0:T(8,128)S(1)}, f32[32,512]{1,0:T(8,128)S(1)}, u32[]{:S(2)}, u32[]{:S(2)}) collective-permute-start(f32[32,512]{1,0:T(8,128)S(1)} %add_add_fusion.after_ref.refs_0_), channel_id=1, source_target_pairs={{0,24},{4,28},{8,16},{12,20},{16,8},{20,12},{24,0},{28,4},{1,25},{... | collective-permute-start | bytes 196616 | tf_op jit(solution)/shard_map/ppermute | solution.py:308
